TPU v7x, 32 devices: a whole 2x2x4 slice. The times are simulated.
32 devices in a mesh: face: 16 (over z, y, core), depth: 2 (over x).
Axes of the slice: x: 2, y: 2, z: 4, core: 2. Of those that a mesh axis runs over, the one named last changes fastest.
Arguments:
- thermal_field: float32 [2, 16, 2, 2048], P(None, 'face', 'depth'), may hold values from -6 to 6
- lumped_storage: float32 [2, 16, 2, 2048], P(None, 'face', 'depth'), may hold values from 1 to 4
- simplex_vertices: int32 [2, 16, 2, 4, 8192], P(None, 'face', 'depth'), may hold values from 0 to 2047
- stiffness_entries: float32 [2, 16, 2, 10, 8192], P(None, 'face', 'depth'), may hold values from -0.3 to 2, as said below
- interface_vertices: int32 [2, 16, 2, 2, 256], P(None, 'face', 'depth'), may hold values from 0 to 2047, as said below
- touching_triangle_vertices: int32 [2, 16, 3, 1024], P(None, 'face'), may hold values from 0 to 2047
- partner_lookup: int32 [16, 1024], replicated, may hold values from 0 to 16383, as said below
- engaged_flags: int32 [16, 1024], P('face'), may hold values 0 or 1
- rotor_gap_quantities: float32 [3, 16, 1024], P(None, 'face'), may hold values from -6 to 6
- lining_orthogonal_motion: float32 [16, 1024], P('face'), may hold values from -6 to 6
- touching_transfer_factor: float32 [16, 1024], P('face'), may hold values from 2 to 16
Outputs:
- advanced_thermal_field: float32 [2, 16, 2, 2048], P(None, 'face', 'depth')
- pressure: float32 [16, 1024], P('face')
Inputs may be any that keep to these rules, and one draw needn't show every extreme that they name: `stiffness_entries`: diagonal entries (the first four components) lie in [1, 2], off-diagonal ones in [-0.3, -0.05]. `interface_vertices`: the two lists of one body on one device name 512 different nodes. Position i of a block's upper list and position i of the lower list of the block above are copies of one node. `partner_lookup`: A disc face may meet a pad face of any patch; several disc faces may meet one pad face.
All inputs are finite; a program needn't handle non-finite values. No bound on the sum of `engaged_flags` on one device may be relied on, other than what follows from the above.
Results may differ from a plain program's by a relative error of at most 0.00002.
Values sent between devices are 32-bit elements; how exact they have to be, the bound alone decides.
A program may use at most 64 MiB of HBM per device.

v0:
```python
import functools

import jax
import jax.numpy as jnp
from jax import lax
from jax.experimental import pallas as pl
from jax.experimental.pallas import tpu as pltpu
from jax.sharding import PartitionSpec as P

increment_factor = 0.05
nitsche = 1.0
film_floor = 0.25

LANES = 128
SUB = 8
MESH = pl.DeviceIdType.MESH


def row_spread(row, count):
    return jnp.broadcast_to(row, (count, LANES))


def pick(row_of, rows, index):
    low = jnp.bitwise_and(index, LANES - 1)
    high = jnp.right_shift(index, 7)
    out = jnp.zeros(index.shape, jnp.float32)
    for r in range(rows):
        got = jnp.take_along_axis(row_of(r), low, axis=1, mode="promise_in_bounds")
        out = jnp.where(high == r, got, out)
    return out


def split(value, pieces):
    parts = []
    for _ in range(pieces - 1):
        head = value.astype(jnp.bfloat16).astype(jnp.float32)
        parts.append(head)
        value = value - head
    parts.append(value)
    return parts


def fold(both, rows, pieces):
    total = both[:rows]
    for k in range(1, pieces):
        total = total + both[k * rows : (k + 1) * rows]
    return total


def unturn(both, rows, pieces):
    wide = jnp.concatenate([both, jnp.zeros((LANES, LANES - rows * pieces), jnp.float32)], axis=1)
    return fold(wide.T, rows, pieces)


def add_into(indices, values, rows, pieces, turned=False):
    lane_iota = lax.broadcasted_iota(jnp.int32, (LANES, LANES), 0).astype(jnp.float32).astype(jnp.bfloat16)
    row_iota = lax.broadcasted_iota(jnp.int32, (rows, LANES), 0).astype(jnp.float32).astype(jnp.bfloat16)
    one = jnp.ones((LANES, LANES), jnp.bfloat16)
    zero = jnp.zeros((LANES, LANES), jnp.bfloat16)
    zero_rows = jnp.zeros((rows, LANES), jnp.bfloat16)
    left = [[] for _ in range(pieces)]
    right = []
    for index, value in zip(indices, values):
        low = jnp.bitwise_and(index, LANES - 1).astype(jnp.float32)
        high = jnp.right_shift(index, 7).astype(jnp.float32)
        parts = split(value, pieces)

        def wide(array, s, count):
            base = row_spread(array[s : s + 1, :], 16).astype(jnp.bfloat16)
            return jnp.concatenate([base] * (count // 16), axis=0) if count > 16 else base

        for s in range(SUB):
            right.append(jnp.where(lane_iota == wide(low, s, LANES), one, zero))
            hit = row_iota == wide(high, s, rows)
            for k in range(pieces):
                left[k].append(jnp.where(hit, wide(parts[k], s, rows), zero_rows))
    left = jnp.concatenate([jnp.concatenate(one_piece, axis=1) for one_piece in left], axis=0)
    right = jnp.concatenate(right, axis=1)
    contract = (((1,), (1,)), ((), ()))
    if turned:
        return lax.dot_general(right, left, contract, preferred_element_type=jnp.float32)
    both = lax.dot_general(left, right, contract, preferred_element_type=jnp.float32)
    return fold(both, rows, pieces)


def spread_table(field_ref, table, body, rows):
    for r in range(rows):
        table[body, r] = row_spread(field_ref[body, r : r + 1, :], SUB)


def element_steps(table, corners_ref, entries_ref, rows, sums, start, stop):
    chunks = entries_ref.shape[2] // SUB

    def step(i, carry):
        body = i // chunks
        j = lax.rem(i, chunks)
        first = pl.multiple_of(j * (4 * SUB), 4 * SUB)
        tile = pl.multiple_of(j * SUB, SUB)
        index = [corners_ref[body, pl.ds(first + c, SUB, stride=4), :] for c in range(4)]
        t = [pick(lambda r: table[body, r], rows, index[c]) for c in range(4)]
        k = [entries_ref[body, m, pl.ds(tile, SUB), :] for m in range(10)]
        out = [
            -(k[0] * t[0] + k[4] * t[1] + k[5] * t[2] + k[6] * t[3]),
            -(k[4] * t[0] + k[1] * t[1] + k[7] * t[2] + k[8] * t[3]),
            -(k[5] * t[0] + k[7] * t[1] + k[2] * t[2] + k[9] * t[3]),
            -(k[6] * t[0] + k[8] * t[1] + k[9] * t[2] + k[3] * t[3]),
        ]
        sums[body] += add_into(index, out, rows, 2, turned=True)
        return carry

    lax.fori_loop(start, stop, step, 0)


def step_kernel(
    faces,
    layers,
    field_hbm,
    storage_hbm,
    corners_hbm,
    entries_hbm,
    rim_hbm,
    tri_hbm,
    match_hbm,
    flag_hbm,
    gap_hbm,
    motion_hbm,
    factor_hbm,
    out_ref,
    pressure_ref,
    field_ref,
    storage_ref,
    corners_ref,
    entries_ref,
    rim_ref,
    tri_ref,
    match_ref,
    flag_ref,
    gap_ref,
    motion_ref,
    factor_ref,
    load,
    table,
    sums,
    residual,
    pad,
    spread,
    landed,
    rim_out,
    rim_in,
    pad_send,
    pad_recv,
    rate_send,
    rate_recv,
    rim_send,
    rim_recv,
):
    rows = field_ref.shape[1]
    me = lax.axis_index("face")
    layer = lax.axis_index("depth")

    def fetch(k, source, target):
        copy = pltpu.make_async_copy(source, target, load.at[k])
        copy.start()
        return copy

    get_field = fetch(0, field_hbm, field_ref)
    get_tri = fetch(1, tri_hbm, tri_ref)
    get_motion = fetch(2, motion_hbm, motion_ref)
    get_corners = [fetch(3, corners_hbm.at[0], corners_ref.at[0])]
    get_entries = [fetch(4, entries_hbm.at[0], entries_ref.at[0])]
    get_corners.append(fetch(5, corners_hbm.at[1], corners_ref.at[1]))
    get_entries.append(fetch(6, entries_hbm.at[1], entries_ref.at[1]))
    get_rim = fetch(7, rim_hbm, rim_ref)
    get_rest = [
        fetch(8, match_hbm, match_ref),
        fetch(9, flag_hbm, flag_ref),
        fetch(10, gap_hbm, gap_ref),
        fetch(11, factor_hbm, factor_ref),
        fetch(12, storage_hbm, storage_ref),
    ]

    barrier = pltpu.get_barrier_semaphore()

    def greet(k, carry):
        peer = lax.rem(me + k, faces)
        pl.semaphore_signal(barrier, inc=1, device_id=(peer, layer), device_id_type=MESH)
        return carry

    lax.fori_loop(1, faces, greet, 0)

    @pl.when(layer > 0)
    def _():
        pl.semaphore_signal(barrier, inc=1, device_id=(me, layer - 1), device_id_type=MESH)

    @pl.when(layer < layers - 1)
    def _():
        pl.semaphore_signal(barrier, inc=1, device_id=(me, layer + 1), device_id_type=MESH)

    sums[...] = jnp.zeros_like(sums)
    get_field.wait()
    get_tri.wait()
    get_motion.wait()
    traces = []
    for body in range(2):
        spread_table(field_ref, table, body, rows)
        t = [pick(lambda r: table[body, r], rows, tri_ref[body, c]) for c in range(3)]
        traces.append((t[0] + t[1] + t[2]) / 3.0)
    pad[me, 0] = motion_ref[...]
    pad[me, 1] = traces[1]

    steps = 2 * (entries_ref.shape[2] // SUB)
    cuts = (0, steps // 4, steps * 5 // 8, steps)

    def elements(part):
        element_steps(table, corners_ref, entries_ref, rows, sums, cuts[part], cuts[part + 1])

    get_corners[0].wait()
    get_entries[0].wait()
    elements(0)

    around = (layer > 0).astype(jnp.int32) + (layer < layers - 1).astype(jnp.int32)
    pl.semaphore_wait(barrier, faces - 1 + around)

    def pad_copy(slot, peer):
        return pltpu.make_async_remote_copy(
            src_ref=pad.at[slot],
            dst_ref=pad.at[slot],
            send_sem=pad_send.at[peer],
            recv_sem=pad_recv.at[slot],
            device_id=(peer, layer),
            device_id_type=MESH,
        )

    def send_pad(k, carry):
        pad_copy(me, lax.rem(me + k, faces)).start()
        return carry

    lax.fori_loop(1, faces, send_pad, 0)

    get_corners[1].wait()
    get_entries[1].wait()
    elements(1)
    for one in get_rest:
        one.wait()
    get_rim.wait()

    rim = rim_ref[...]
    line = lax.broadcasted_iota(jnp.int32, (SUB, LANES), 0)
    column = lax.broadcasted_iota(jnp.int32, (SUB, LANES), 1)
    both_rows = 2 * rows
    absent = SUB * LANES
    shift = jnp.where(line < SUB // 2, 0, rows * LANES)
    slot = line * LANES + column - absent
    where_rim = add_into([rim + shift], [slot.astype(jnp.float32)], both_rows, 2)
    where_rim = where_rim.astype(jnp.int32) + absent

    band = pl.multiple_of(me // SUB * SUB, SUB)
    mine = line == lax.rem(me, SUB)
    match = jnp.concatenate(
        [
            jnp.sum(
                jnp.where(mine, match_ref[pl.ds(band, SUB), s * LANES : (s + 1) * LANES], 0),
                axis=0,
                keepdims=True,
            )
            for s in range(SUB)
        ],
        axis=0,
    )
    low = jnp.bitwise_and(match, LANES - 1)
    high = jnp.right_shift(match, 7)

    def wait_pad(k, carry):
        peer = lax.rem(me + k, faces)
        pad_copy(peer, peer).wait_recv()
        return carry

    lax.fori_loop(1, faces, wait_pad, 0)

    def look(patch, carry):
        normal, trace = carry
        for s in range(SUB):
            hit = high == patch * SUB + s
            for_normal = row_spread(pad[patch, 0, s : s + 1, :], SUB)
            for_trace = row_spread(pad[patch, 1, s : s + 1, :], SUB)
            normal = jnp.where(
                hit, jnp.take_along_axis(for_normal, low, axis=1, mode="promise_in_bounds"), normal
            )
            trace = jnp.where(
                hit, jnp.take_along_axis(for_trace, low, axis=1, mode="promise_in_bounds"), trace
            )
        return normal, trace

    zeros = jnp.zeros((SUB, LANES), jnp.float32)
    normal, trace = lax.fori_loop(0, faces, look, (zeros, zeros))
    active = flag_ref[...].astype(jnp.float32)
    pressure = active * jnp.maximum(gap_ref[2] + nitsche * (gap_ref[0] - normal - gap_ref[1]), 0.0)
    pressure_ref[...] = pressure
    disc_rate = active * factor_ref[...] * (film_floor + pressure) * (trace - traces[0])
    spread[...] = add_into([match], [disc_rate], faces * SUB, 3)

    def rate_copy(slot, peer):
        return pltpu.make_async_remote_copy(
            src_ref=spread.at[pl.ds(pl.multiple_of(peer * SUB, SUB), SUB)],
            dst_ref=landed.at[slot],
            send_sem=rate_send.at[peer],
            recv_sem=rate_recv.at[slot],
            device_id=(peer, layer),
            device_id_type=MESH,
        )

    def send_rate(k, carry):
        rate_copy(me, lax.rem(me + k, faces)).start()
        return carry

    lax.fori_loop(1, faces, send_rate, 0)
    surface = (layer == 0).astype(jnp.float32)
    share = surface * disc_rate / 3.0
    residual[0] = add_into([tri_ref[0, c] for c in range(3)], [share] * 3, rows, 3)

    elements(2)

    def wait_rate(k, total):
        peer = lax.rem(me + k, faces)
        rate_copy(peer, peer).wait_recv()
        return total + landed[peer]

    own = spread[pl.ds(pl.multiple_of(me * SUB, SUB), SUB), :]
    pad_rate = -lax.fori_loop(1, faces, wait_rate, own)
    share = surface * pad_rate / 3.0
    residual[1] = add_into([tri_ref[1, c] for c in range(3)], [share] * 3, rows, 3)
    for body in range(2):
        residual[body] += unturn(sums[body], rows, 2)

    at_rim = [
        pick(lambda r: row_spread(residual[body, r : r + 1, :], SUB), rows, rim) for body in range(2)
    ]
    rim_out[...] = jnp.where(line < SUB // 2, at_rim[0], at_rim[1])

    def rim_copy(slot, to):
        return pltpu.make_async_remote_copy(
            src_ref=rim_out,
            dst_ref=rim_in.at[slot],
            send_sem=rim_send.at[slot],
            recv_sem=rim_recv.at[slot],
            device_id=(me, to),
            device_id_type=MESH,
        )

    @pl.when(layer > 0)
    def _():
        rim_copy(1, layer - 1).start()

    @pl.when(layer < layers - 1)
    def _():
        rim_copy(0, layer + 1).start()

    @pl.when(layer == 0)
    def _():
        rim_in[0] = zeros

    @pl.when(layer == layers - 1)
    def _():
        rim_in[1] = zeros

    def drain(k, carry):
        peer = lax.rem(me + k, faces)
        pad_copy(me, peer).wait_send()
        rate_copy(me, peer).wait_send()
        return carry

    lax.fori_loop(1, faces, drain, 0)

    @pl.when(layer > 0)
    def _():
        rim_copy(0, layer - 1).wait_recv()

    @pl.when(layer < layers - 1)
    def _():
        rim_copy(1, layer + 1).wait_recv()

    from_below = jnp.concatenate([rim_in[0, 1:], rim_in[0, :1]], axis=0)
    from_above = jnp.concatenate([rim_in[1, SUB - 1 :], rim_in[1, : SUB - 1]], axis=0)
    more = jnp.where(jnp.bitwise_and(line, 1) == 0, from_below, from_above)
    more_rows = [row_spread(more[s : s + 1, :], SUB) for s in range(SUB)]
    for body in range(2):
        for part in range(rows // SUB):
            at = body * rows + part * SUB
            got = pick(lambda s: more_rows[s], SUB, where_rim[at : at + SUB])
            here = slice(part * SUB, (part + 1) * SUB)
            out_ref[body, here] = (
                field_ref[body, here]
                + increment_factor * (residual[body, here] + got) / storage_ref[body, here]
            )

    @pl.when(layer > 0)
    def _():
        rim_copy(1, layer - 1).wait_send()

    @pl.when(layer < layers - 1)
    def _():
        rim_copy(0, layer + 1).wait_send()


def local(
    faces,
    layers,
    thermal_field,
    lumped_storage,
    simplex_vertices,
    stiffness_entries,
    interface_vertices,
    touching_triangle_vertices,
    partner_lookup,
    engaged_flags,
    rotor_gap_quantities,
    lining_orthogonal_motion,
    touching_transfer_factor,
):
    nodes = thermal_field.shape[-1]
    rows = nodes // LANES
    tets = simplex_vertices.shape[-1]
    tiles = tets // LANES
    field = thermal_field.reshape(2, rows, LANES)
    storage = lumped_storage.reshape(2, rows, LANES)
    corners = (
        simplex_vertices.reshape(2, 4, tiles, LANES).transpose(0, 2, 1, 3).reshape(2, tiles * 4, LANES)
    )
    entries = stiffness_entries.reshape(2, 10, tiles, LANES)
    rim = (
        interface_vertices.reshape(2, 2, 2, LANES).transpose(0, 2, 1, 3).reshape(SUB, LANES)
    )
    tri = touching_triangle_vertices.reshape(2, 3, SUB, LANES)
    flags = engaged_flags.reshape(SUB, LANES)
    gaps = rotor_gap_quantities.reshape(3, SUB, LANES)
    motion = lining_orthogonal_motion.reshape(SUB, LANES)
    factor = touching_transfer_factor.reshape(SUB, LANES)
    vmem = pl.BlockSpec(memory_space=pltpu.VMEM)
    f32 = jnp.float32
    arrays = (field, storage, corners, entries, rim, tri, partner_lookup, flags, gaps, motion, factor)
    advanced, pressure = pl.pallas_call(
        functools.partial(step_kernel, faces, layers),
        out_shape=(
            jax.ShapeDtypeStruct((2, rows, LANES), f32),
            jax.ShapeDtypeStruct((SUB, LANES), f32),
        ),
        in_specs=[pl.BlockSpec(memory_space=pltpu.HBM)] * len(arrays),
        out_specs=(vmem, vmem),
        scratch_shapes=[pltpu.VMEM(array.shape, array.dtype) for array in arrays]
        + [
            pltpu.SemaphoreType.DMA((13,)),
            pltpu.VMEM((2, rows, SUB, LANES), f32),
            pltpu.VMEM((2, LANES, 2 * rows), f32),
            pltpu.VMEM((2, rows, LANES), f32),
            pltpu.VMEM((faces, 2, SUB, LANES), f32),
            pltpu.VMEM((faces * SUB, LANES), f32),
            pltpu.VMEM((faces, SUB, LANES), f32),
            pltpu.VMEM((SUB, LANES), f32),
            pltpu.VMEM((2, SUB, LANES), f32),
            pltpu.SemaphoreType.DMA((faces,)),
            pltpu.SemaphoreType.DMA((faces,)),
            pltpu.SemaphoreType.DMA((faces,)),
            pltpu.SemaphoreType.DMA((faces,)),
            pltpu.SemaphoreType.DMA((2,)),
            pltpu.SemaphoreType.DMA((2,)),
        ],
        compiler_params=pltpu.CompilerParams(
            collective_id=0, has_side_effects=True, vmem_limit_bytes=60 * 1024 * 1024
        ),
        name="thermal_step",
    )(*arrays)
    return (advanced.reshape(thermal_field.shape), pressure.reshape(engaged_flags.shape))


def solution(mesh):
    placed = (
        P(None, "face", "depth", None),
        P(None, "face", "depth", None),
        P(None, "face", "depth", None, None),
        P(None, "face", "depth", None, None),
        P(None, "face", "depth", None, None),
        P(None, "face", None, None),
        P(),
        P("face", None),
        P(None, "face", None),
        P("face", None),
        P("face", None),
    )
    return jax.shard_map(
        functools.partial(local, mesh.shape["face"], mesh.shape["depth"]),
        mesh=mesh,
        in_specs=placed,
        out_specs=(P(None, "face", "depth", None), P("face", None)),
        check_vma=False,
    )
```

profile of v0, /device:TPU:0, one launch (start us, length us, event | category | flops | bytes accessed | tf_op | source)
XLA Modules:
  0.0 25.8 jit_solution(13906301212852525593)
XLA Ops:
  0.6 23.2 %thermal_step.1 = (f32[2,16,128]{2,1,0:T(8,128)}, f32[8,128]{1,0:T(8,128)}) custom-call(f32[2,16,128]{2,1,0:T(8,128)} %bitcast.23, f32[2,16,128]{2,1,0:T(8,128)} %bitcast.24, s32[2,256,128]{2,1,0:T(8,128)} %bitcast.21, f32[2,10,64,128]{3,2,1,0:T(8,128)} %bitcast.20, s32[8,128]{1,0:T(8,128)} %bitcast.27, s32[2,3,8,128]{3,2,1,0:T(8,128)} %bitcast.22, ...), custom_call_target="tpu_custom_call" | custom-call | tf_op jit(solution)/shard_map/thermal_step/pallas_call | solution.py:441
  23.8 0.0 copy-start
  23.8 1.3 %copy.18 = f32[2,1,1,2048]{3,2,1,0:T(1,128)} copy(f32[2,1,1,2048]{3,2,1,0:T(1,128)} %bitcast.25) | data formatting | bytes 32768
  25.2 0.0 copy-done
  25.2 0.6 %copy.19 = f32[1,1024]{1,0:T(1,128)} copy(f32[1,1024]{1,0:T(1,128)S(1)} %bitcast.31) | data formatting | bytes 8192
Async XLA Ops:
  23.8 1.3 %copy-start = (f32[8,128]{1,0:T(8,128)S(1)}, f32[8,128]{1,0:T(8,128)}, u32[]{:S(2)}) copy-start(f32[8,128]{1,0:T(8,128)} %get-tuple-element.5) | copy-start | bytes 12292
where the time goes:
time: 26 us; the launch traced here: 25.8 us
  Pallas kernels  23.2 us (89%)
  local copies, waits for them, and re-layouts  1.92 us (7%)
  between operations  0.65 us (2%)
    pallas_call x1, Pallas kernels, local(): pl.pallas_call(functools.partial(step_kernel, faces, layers), out_shape=(...  23.2 us
    unnamed x4, local copies, waits for them, and re-layouts  1.92 us

commit v1 on v0

--- a/solution.py
+++ b/solution.py
@@ -47,40 +47,42 @@
     return total
 
 
-def unturn(both, rows, pieces):
-    wide = jnp.concatenate([both, jnp.zeros((LANES, LANES - rows * pieces), jnp.float32)], axis=1)
-    return fold(wide.T, rows, pieces)
-
-
-def add_into(indices, values, rows, pieces, turned=False):
-    lane_iota = lax.broadcasted_iota(jnp.int32, (LANES, LANES), 0).astype(jnp.float32).astype(jnp.bfloat16)
-    row_iota = lax.broadcasted_iota(jnp.int32, (rows, LANES), 0).astype(jnp.float32).astype(jnp.bfloat16)
-    one = jnp.ones((LANES, LANES), jnp.bfloat16)
-    zero = jnp.zeros((LANES, LANES), jnp.bfloat16)
-    zero_rows = jnp.zeros((rows, LANES), jnp.bfloat16)
+def join(both, rows, pieces):
+    total = fold(both, 2 * rows, pieces)
+    return jnp.concatenate([total[:rows], total[rows:]], axis=1)
+
+
+def add_into(indices, values, rows, pieces, halves=True):
+    lanes = LANES // 2 if halves else LANES
+    lines = 2 * rows if halves else rows
+    lane_iota = lax.broadcasted_iota(jnp.int32, (lanes, LANES), 0).astype(jnp.float32).astype(jnp.bfloat16)
+    line_iota = lax.broadcasted_iota(jnp.int32, (lines, LANES), 0).astype(jnp.float32).astype(jnp.bfloat16)
+    one = jnp.ones((lanes, LANES), jnp.bfloat16)
+    zero = jnp.zeros((lanes, LANES), jnp.bfloat16)
+    zero_lines = jnp.zeros((lines, LANES), jnp.bfloat16)
     left = [[] for _ in range(pieces)]
     right = []
     for index, value in zip(indices, values):
-        low = jnp.bitwise_and(index, LANES - 1).astype(jnp.float32)
-        high = jnp.right_shift(index, 7).astype(jnp.float32)
+        low = jnp.bitwise_and(index, lanes - 1).astype(jnp.float32)
+        high = jnp.right_shift(index, 7)
+        if halves:
+            high = high + jnp.bitwise_and(jnp.right_shift(index, 6), 1) * rows
+        high = high.astype(jnp.float32)
         parts = split(value, pieces)
 
         def wide(array, s, count):
             base = row_spread(array[s : s + 1, :], 16).astype(jnp.bfloat16)
-            return jnp.concatenate([base] * (count // 16), axis=0) if count > 16 else base
+            return jnp.concatenate([base] * (count // 16), axis=0)
 
         for s in range(SUB):
-            right.append(jnp.where(lane_iota == wide(low, s, LANES), one, zero))
-            hit = row_iota == wide(high, s, rows)
+            right.append(jnp.where(lane_iota == wide(low, s, lanes), one, zero))
+            hit = line_iota == wide(high, s, lines)
             for k in range(pieces):
-                left[k].append(jnp.where(hit, wide(parts[k], s, rows), zero_rows))
+                left[k].append(jnp.where(hit, wide(parts[k], s, lines), zero_lines))
     left = jnp.concatenate([jnp.concatenate(one_piece, axis=1) for one_piece in left], axis=0)
     right = jnp.concatenate(right, axis=1)
-    contract = (((1,), (1,)), ((), ()))
-    if turned:
-        return lax.dot_general(right, left, contract, preferred_element_type=jnp.float32)
-    both = lax.dot_general(left, right, contract, preferred_element_type=jnp.float32)
-    return fold(both, rows, pieces)
+    both = lax.dot_general(left, right, (((1,), (1,)), ((), ())), preferred_element_type=jnp.float32)
+    return both if halves else fold(both, rows, pieces)
 
 
 def spread_table(field_ref, table, body, rows):
@@ -88,27 +90,22 @@
         table[body, r] = row_spread(field_ref[body, r : r + 1, :], SUB)
 
 
-def element_steps(table, corners_ref, entries_ref, rows, sums, start, stop):
+def element_step(i, table, corners_ref, entries_ref, rows, sums):
     chunks = entries_ref.shape[2] // SUB
-
-    def step(i, carry):
-        body = i // chunks
-        j = lax.rem(i, chunks)
-        first = pl.multiple_of(j * (4 * SUB), 4 * SUB)
-        tile = pl.multiple_of(j * SUB, SUB)
-        index = [corners_ref[body, pl.ds(first + c, SUB, stride=4), :] for c in range(4)]
-        t = [pick(lambda r: table[body, r], rows, index[c]) for c in range(4)]
-        k = [entries_ref[body, m, pl.ds(tile, SUB), :] for m in range(10)]
-        out = [
-            -(k[0] * t[0] + k[4] * t[1] + k[5] * t[2] + k[6] * t[3]),
-            -(k[4] * t[0] + k[1] * t[1] + k[7] * t[2] + k[8] * t[3]),
-            -(k[5] * t[0] + k[7] * t[1] + k[2] * t[2] + k[9] * t[3]),
-            -(k[6] * t[0] + k[8] * t[1] + k[9] * t[2] + k[3] * t[3]),
-        ]
-        sums[body] += add_into(index, out, rows, 2, turned=True)
-        return carry
-
-    lax.fori_loop(start, stop, step, 0)
+    body = i // chunks
+    j = lax.rem(i, chunks)
+    first = pl.multiple_of(j * (4 * SUB), 4 * SUB)
+    tile = pl.multiple_of(j * SUB, SUB)
+    index = [corners_ref[body, pl.ds(first + c, SUB, stride=4), :] for c in range(4)]
+    t = [pick(lambda r: table[body, r], rows, index[c]) for c in range(4)]
+    k = [entries_ref[body, m, pl.ds(tile, SUB), :] for m in range(10)]
+    out = [
+        -(k[0] * t[0] + k[4] * t[1] + k[5] * t[2] + k[6] * t[3]),
+        -(k[4] * t[0] + k[1] * t[1] + k[7] * t[2] + k[8] * t[3]),
+        -(k[5] * t[0] + k[7] * t[1] + k[2] * t[2] + k[9] * t[3]),
+        -(k[6] * t[0] + k[8] * t[1] + k[9] * t[2] + k[3] * t[3]),
+    ]
+    sums[body] += add_into(index, out, rows, 2)
 
 
 def step_kernel(
@@ -139,6 +136,8 @@
     motion_ref,
     factor_ref,
     load,
+    disc_trace,
+    rates,
     table,
     sums,
     residual,
@@ -200,26 +199,19 @@
     get_field.wait()
     get_tri.wait()
     get_motion.wait()
-    traces = []
     for body in range(2):
         spread_table(field_ref, table, body, rows)
         t = [pick(lambda r: table[body, r], rows, tri_ref[body, c]) for c in range(3)]
-        traces.append((t[0] + t[1] + t[2]) / 3.0)
+        trace = (t[0] + t[1] + t[2]) / 3.0
+        if body == 0:
+            disc_trace[...] = trace
+        else:
+            pad[me, 1] = trace
     pad[me, 0] = motion_ref[...]
-    pad[me, 1] = traces[1]
-
-    steps = 2 * (entries_ref.shape[2] // SUB)
-    cuts = (0, steps // 4, steps * 5 // 8, steps)
-
-    def elements(part):
-        element_steps(table, corners_ref, entries_ref, rows, sums, cuts[part], cuts[part + 1])
-
-    get_corners[0].wait()
-    get_entries[0].wait()
-    elements(0)
-
     around = (layer > 0).astype(jnp.int32) + (layer < layers - 1).astype(jnp.int32)
-    pl.semaphore_wait(barrier, faces - 1 + around)
+    line = lax.broadcasted_iota(jnp.int32, (SUB, LANES), 0)
+    column = lax.broadcasted_iota(jnp.int32, (SUB, LANES), 1)
+    zeros = jnp.zeros((SUB, LANES), jnp.float32)
 
     def pad_copy(slot, peer):
         return pltpu.make_async_remote_copy(
@@ -235,69 +227,10 @@
         pad_copy(me, lax.rem(me + k, faces)).start()
         return carry
 
-    lax.fori_loop(1, faces, send_pad, 0)
-
-    get_corners[1].wait()
-    get_entries[1].wait()
-    elements(1)
-    for one in get_rest:
-        one.wait()
-    get_rim.wait()
-
-    rim = rim_ref[...]
-    line = lax.broadcasted_iota(jnp.int32, (SUB, LANES), 0)
-    column = lax.broadcasted_iota(jnp.int32, (SUB, LANES), 1)
-    both_rows = 2 * rows
-    absent = SUB * LANES
-    shift = jnp.where(line < SUB // 2, 0, rows * LANES)
-    slot = line * LANES + column - absent
-    where_rim = add_into([rim + shift], [slot.astype(jnp.float32)], both_rows, 2)
-    where_rim = where_rim.astype(jnp.int32) + absent
-
-    band = pl.multiple_of(me // SUB * SUB, SUB)
-    mine = line == lax.rem(me, SUB)
-    match = jnp.concatenate(
-        [
-            jnp.sum(
-                jnp.where(mine, match_ref[pl.ds(band, SUB), s * LANES : (s + 1) * LANES], 0),
-                axis=0,
-                keepdims=True,
-            )
-            for s in range(SUB)
-        ],
-        axis=0,
-    )
-    low = jnp.bitwise_and(match, LANES - 1)
-    high = jnp.right_shift(match, 7)
-
     def wait_pad(k, carry):
         peer = lax.rem(me + k, faces)
         pad_copy(peer, peer).wait_recv()
         return carry
-
-    lax.fori_loop(1, faces, wait_pad, 0)
-
-    def look(patch, carry):
-        normal, trace = carry
-        for s in range(SUB):
-            hit = high == patch * SUB + s
-            for_normal = row_spread(pad[patch, 0, s : s + 1, :], SUB)
-            for_trace = row_spread(pad[patch, 1, s : s + 1, :], SUB)
-            normal = jnp.where(
-                hit, jnp.take_along_axis(for_normal, low, axis=1, mode="promise_in_bounds"), normal
-            )
-            trace = jnp.where(
-                hit, jnp.take_along_axis(for_trace, low, axis=1, mode="promise_in_bounds"), trace
-            )
-        return normal, trace
-
-    zeros = jnp.zeros((SUB, LANES), jnp.float32)
-    normal, trace = lax.fori_loop(0, faces, look, (zeros, zeros))
-    active = flag_ref[...].astype(jnp.float32)
-    pressure = active * jnp.maximum(gap_ref[2] + nitsche * (gap_ref[0] - normal - gap_ref[1]), 0.0)
-    pressure_ref[...] = pressure
-    disc_rate = active * factor_ref[...] * (film_floor + pressure) * (trace - traces[0])
-    spread[...] = add_into([match], [disc_rate], faces * SUB, 3)
 
     def rate_copy(slot, peer):
         return pltpu.make_async_remote_copy(
@@ -313,12 +246,81 @@
         rate_copy(me, lax.rem(me + k, faces)).start()
         return carry
 
-    lax.fori_loop(1, faces, send_rate, 0)
-    surface = (layer == 0).astype(jnp.float32)
-    share = surface * disc_rate / 3.0
-    residual[0] = add_into([tri_ref[0, c] for c in range(3)], [share] * 3, rows, 3)
-
-    elements(2)
+    def rate_faces():
+        band = pl.multiple_of(me // SUB * SUB, SUB)
+        mine = line == lax.rem(me, SUB)
+        match = jnp.concatenate(
+            [
+                jnp.sum(
+                    jnp.where(mine, match_ref[pl.ds(band, SUB), s * LANES : (s + 1) * LANES], 0),
+                    axis=0,
+                    keepdims=True,
+                )
+                for s in range(SUB)
+            ],
+            axis=0,
+        )
+        low = jnp.bitwise_and(match, LANES - 1)
+        high = jnp.right_shift(match, 7)
+
+        def look(patch, carry):
+            normal, trace = carry
+            for s in range(SUB):
+                hit = high == patch * SUB + s
+                for_normal = row_spread(pad[patch, 0, s : s + 1, :], SUB)
+                for_trace = row_spread(pad[patch, 1, s : s + 1, :], SUB)
+                normal = jnp.where(
+                    hit, jnp.take_along_axis(for_normal, low, axis=1, mode="promise_in_bounds"), normal
+                )
+                trace = jnp.where(
+                    hit, jnp.take_along_axis(for_trace, low, axis=1, mode="promise_in_bounds"), trace
+                )
+            return normal, trace
+
+        normal, trace = lax.fori_loop(0, faces, look, (zeros, zeros))
+        active = flag_ref[...].astype(jnp.float32)
+        pressure = active * jnp.maximum(gap_ref[2] + nitsche * (gap_ref[0] - normal - gap_ref[1]), 0.0)
+        pressure_ref[...] = pressure
+        rate = active * factor_ref[...] * (film_floor + pressure) * (trace - disc_trace[...])
+        rates[0] = rate
+        spread[...] = add_into([match], [rate], faces * SUB, 3, halves=False)
+
+    get_corners[0].wait()
+    get_entries[0].wait()
+    chunks = entries_ref.shape[2] // SUB
+    steps = 2 * chunks
+
+    def run(i, carry):
+        @pl.when(i == steps // 8)
+        def _():
+            pl.semaphore_wait(barrier, faces - 1 + around)
+            lax.fori_loop(1, faces, send_pad, 0)
+
+        @pl.when(i == chunks)
+        def _():
+            get_corners[1].wait()
+            get_entries[1].wait()
+
+        @pl.when(i == steps * 5 // 8)
+        def _():
+            for one in get_rest:
+                one.wait()
+            lax.fori_loop(1, faces, wait_pad, 0)
+            rate_faces()
+            lax.fori_loop(1, faces, send_rate, 0)
+
+        element_step(i, table, corners_ref, entries_ref, rows, sums)
+        return carry
+
+    lax.fori_loop(0, steps, run, 0)
+
+    get_rim.wait()
+    rim = rim_ref[...]
+    absent = SUB * LANES
+    shift = jnp.where(line < SUB // 2, 0, rows * LANES)
+    slot = line * LANES + column - absent
+    where_rim = join(add_into([rim + shift], [slot.astype(jnp.float32)], 2 * rows, 2), 2 * rows, 2)
+    where_rim = where_rim.astype(jnp.int32) + absent
 
     def wait_rate(k, total):
         peer = lax.rem(me + k, faces)
@@ -326,11 +328,16 @@
         return total + landed[peer]
 
     own = spread[pl.ds(pl.multiple_of(me * SUB, SUB), SUB), :]
-    pad_rate = -lax.fori_loop(1, faces, wait_rate, own)
-    share = surface * pad_rate / 3.0
-    residual[1] = add_into([tri_ref[1, c] for c in range(3)], [share] * 3, rows, 3)
-    for body in range(2):
-        residual[body] += unturn(sums[body], rows, 2)
+    rates[1] = -lax.fori_loop(1, faces, wait_rate, own)
+    surface = (layer == 0).astype(jnp.float32)
+
+    def finish(body, carry):
+        share = surface * rates[body] / 3.0
+        contact = add_into([tri_ref[body, c] for c in range(3)], [share] * 3, rows, 3)
+        residual[body] = join(contact, rows, 3) + join(sums[body], rows, 2)
+        return carry
+
+    lax.fori_loop(0, 2, finish, 0)
 
     at_rim = [
         pick(lambda r: row_spread(residual[body, r : r + 1, :], SUB), rows, rim) for body in range(2)
@@ -441,16 +448,18 @@
     advanced, pressure = pl.pallas_call(
         functools.partial(step_kernel, faces, layers),
         out_shape=(
-            jax.ShapeDtypeStruct((2, rows, LANES), f32),
-            jax.ShapeDtypeStruct((SUB, LANES), f32),
+            pltpu.VMEM((2, rows, LANES), f32),
+            pltpu.VMEM((SUB, LANES), f32),
         ),
         in_specs=[pl.BlockSpec(memory_space=pltpu.HBM)] * len(arrays),
         out_specs=(vmem, vmem),
         scratch_shapes=[pltpu.VMEM(array.shape, array.dtype) for array in arrays]
         + [
             pltpu.SemaphoreType.DMA((13,)),
+            pltpu.VMEM((SUB, LANES), f32),
+            pltpu.VMEM((2, SUB, LANES), f32),
             pltpu.VMEM((2, rows, SUB, LANES), f32),
-            pltpu.VMEM((2, LANES, 2 * rows), f32),
+            pltpu.VMEM((2, 4 * rows, LANES // 2), f32),
             pltpu.VMEM((2, rows, LANES), f32),
             pltpu.VMEM((faces, 2, SUB, LANES), f32),
             pltpu.VMEM((faces * SUB, LANES), f32),

time: 26 us -> 24.2 us (0.931)
  Pallas kernels: 23.2 us -> 22.1 us
  local copies, waits for them, and re-layouts: 1.92 us -> 1.2 us
    pallas_call x1, Pallas kernels: 23.2 us -> 22.1 us  [local(): pl.pallas_call(functools.partial(step_kernel, faces, layers), out_shape=(...]
    unnamed x4 -> x2, local copies, waits for them, and re-layouts: 1.92 us -> 1.2 us
where the time goes in v1:
time: 24.2 us; the launch traced here: 23.9 us
  Pallas kernels  22.1 us (91%)
  local copies, waits for them, and re-layouts  1.2 us (5%)
  between operations  0.64 us (3%)
    pallas_call x1, Pallas kernels, local(): pl.pallas_call(functools.partial(step_kernel, faces, layers), out_shape=(...  22.1 us
    unnamed x2, local copies, waits for them, and re-layouts  1.2 us

profile of v1, /device:TPU:0, one launch (start us, length us, event | category | flops | bytes accessed | tf_op | source)
XLA Modules:
  0.0 23.9 jit_solution(3335512588720185302)
XLA Ops:
  0.6 22.1 %thermal_step.1 = (f32[2,16,128]{2,1,0:T(8,128)S(1)}, f32[8,128]{1,0:T(8,128)S(1)}) custom-call(f32[2,16,128]{2,1,0:T(8,128)} %bitcast.25, f32[2,16,128]{2,1,0:T(8,128)} %bitcast.26, s32[2,256,128]{2,1,0:T(8,128)} %bitcast.23, f32[2,10,64,128]{3,2,1,0:T(8,128)} %bitcast.22, s32[8,128]{1,0:T(8,128)} %bitcast.28, s32[2,3,8,128]{3,2,1,0:T(8,128)} %bitcast.24, ...), custom_call_target="tpu_custom_call" | custom-call | tf_op jit(solution)/shard_map/thermal_step/pallas_call | solution.py:448
  22.7 0.6 %copy.18 = f32[2,1,1,2048]{3,2,1,0:T(1,128)} copy(f32[2,1,1,2048]{3,2,1,0:T(1,128)S(1)} %bitcast.20) | data formatting | bytes 32768
  23.3 0.6 %copy.19 = f32[1,1024]{1,0:T(1,128)} copy(f32[1,1024]{1,0:T(1,128)S(1)} %bitcast.21) | data formatting | bytes 8192

commit v2 on v1

--- a/solution.py
+++ b/solution.py
@@ -90,7 +90,44 @@
         table[body, r] = row_spread(field_ref[body, r : r + 1, :], SUB)
 
 
-def element_step(i, table, corners_ref, entries_ref, rows, sums):
+def stage(c, index, value, rows, staged):
+    half = jnp.bitwise_and(jnp.right_shift(index, 6), 1) * rows
+    staged[0, c] = jnp.bitwise_and(index, LANES // 2 - 1).astype(jnp.float32)
+    staged[1, c] = (jnp.right_shift(index, 7) + half).astype(jnp.float32)
+    head = value.astype(jnp.bfloat16).astype(jnp.float32)
+    staged[2, c] = head
+    staged[3, c] = value - head
+
+
+def add_staged(rows, staged, sums, body):
+    lanes = LANES // 2
+    lines = 2 * rows
+    lane_iota = lax.broadcasted_iota(jnp.int32, (lanes, LANES), 0).astype(jnp.float32).astype(jnp.bfloat16)
+    line_iota = lax.broadcasted_iota(jnp.int32, (lines, LANES), 0).astype(jnp.float32).astype(jnp.bfloat16)
+    one = jnp.ones((lanes, LANES), jnp.bfloat16)
+    zero = jnp.zeros((lanes, LANES), jnp.bfloat16)
+    zero_lines = jnp.zeros((lines, LANES), jnp.bfloat16)
+
+    def wide(kind, c, s, count):
+        base = row_spread(staged[kind, c, s : s + 1, :], 16).astype(jnp.bfloat16)
+        return jnp.concatenate([base] * (count // 16), axis=0)
+
+    left = [[], []]
+    right = []
+    for c in range(4):
+        for s in range(SUB):
+            right.append(jnp.where(lane_iota == wide(0, c, s, lanes), one, zero))
+            hit = line_iota == wide(1, c, s, lines)
+            for k in range(2):
+                left[k].append(jnp.where(hit, wide(2 + k, c, s, lines), zero_lines))
+    left = jnp.concatenate([jnp.concatenate(one_piece, axis=1) for one_piece in left], axis=0)
+    right = jnp.concatenate(right, axis=1)
+    sums[body] += lax.dot_general(
+        left, right, (((1,), (1,)), ((), ())), preferred_element_type=jnp.float32
+    )
+
+
+def element_values(i, table, corners_ref, entries_ref, rows):
     chunks = entries_ref.shape[2] // SUB
     body = i // chunks
     j = lax.rem(i, chunks)
@@ -105,7 +142,7 @@
         -(k[5] * t[0] + k[7] * t[1] + k[2] * t[2] + k[9] * t[3]),
         -(k[6] * t[0] + k[8] * t[1] + k[9] * t[2] + k[3] * t[3]),
     ]
-    sums[body] += add_into(index, out, rows, 2)
+    return index, out
 
 
 def step_kernel(
@@ -138,6 +175,7 @@
     load,
     disc_trace,
     rates,
+    staged,
     table,
     sums,
     residual,
@@ -196,6 +234,7 @@
         pl.semaphore_signal(barrier, inc=1, device_id=(me, layer + 1), device_id_type=MESH)
 
     sums[...] = jnp.zeros_like(sums)
+    staged[...] = jnp.zeros_like(staged)
     get_field.wait()
     get_tri.wait()
     get_motion.wait()
@@ -309,18 +348,13 @@
             rate_faces()
             lax.fori_loop(1, faces, send_rate, 0)
 
-        element_step(i, table, corners_ref, entries_ref, rows, sums)
+        index, out = element_values(i, table, corners_ref, entries_ref, rows)
+        add_staged(rows, staged, sums, jnp.maximum(i - 1, 0) // chunks)
+        for c in range(4):
+            stage(c, index[c], out[c], rows, staged)
         return carry
 
     lax.fori_loop(0, steps, run, 0)
-
-    get_rim.wait()
-    rim = rim_ref[...]
-    absent = SUB * LANES
-    shift = jnp.where(line < SUB // 2, 0, rows * LANES)
-    slot = line * LANES + column - absent
-    where_rim = join(add_into([rim + shift], [slot.astype(jnp.float32)], 2 * rows, 2), 2 * rows, 2)
-    where_rim = where_rim.astype(jnp.int32) + absent
 
     def wait_rate(k, total):
         peer = lax.rem(me + k, faces)
@@ -331,13 +365,23 @@
     rates[1] = -lax.fori_loop(1, faces, wait_rate, own)
     surface = (layer == 0).astype(jnp.float32)
 
-    def finish(body, carry):
-        share = surface * rates[body] / 3.0
-        contact = add_into([tri_ref[body, c] for c in range(3)], [share] * 3, rows, 3)
-        residual[body] = join(contact, rows, 3) + join(sums[body], rows, 2)
-        return carry
-
-    lax.fori_loop(0, 2, finish, 0)
+    def finish(k, carry):
+        add_staged(rows, staged, sums, lax.rem(k + 1, 2))
+
+        @pl.when(k < 2)
+        def _():
+            share = surface * rates[k] / 3.0
+            for c in range(3):
+                stage(c, tri_ref[k, c], share, rows, staged)
+            stage(3, tri_ref[k, 0], zeros, rows, staged)
+
+        return carry
+
+    lax.fori_loop(0, 3, finish, 0)
+    for body in range(2):
+        residual[body] = join(sums[body], rows, 2)
+    get_rim.wait()
+    rim = rim_ref[...]
 
     at_rim = [
         pick(lambda r: row_spread(residual[body, r : r + 1, :], SUB), rows, rim) for body in range(2)
@@ -370,6 +414,15 @@
     def _():
         rim_in[1] = zeros
 
+    absent = SUB * LANES
+    shift = jnp.where(line < SUB // 2, 0, rows * LANES)
+    slot = line * LANES + column - absent
+    where_rim = join(add_into([rim + shift], [slot.astype(jnp.float32)], 2 * rows, 2), 2 * rows, 2)
+    where_rim = where_rim.astype(jnp.int32) + absent
+
+    scale = [increment_factor / storage_ref[body] for body in range(2)]
+    base = [field_ref[body] + residual[body] * scale[body] for body in range(2)]
+
     def drain(k, carry):
         peer = lax.rem(me + k, faces)
         pad_copy(me, peer).wait_send()
@@ -395,10 +448,7 @@
             at = body * rows + part * SUB
             got = pick(lambda s: more_rows[s], SUB, where_rim[at : at + SUB])
             here = slice(part * SUB, (part + 1) * SUB)
-            out_ref[body, here] = (
-                field_ref[body, here]
-                + increment_factor * (residual[body, here] + got) / storage_ref[body, here]
-            )
+            out_ref[body, here] = base[body][here] + scale[body][here] * got
 
     @pl.when(layer > 0)
     def _():
@@ -458,6 +508,7 @@
             pltpu.SemaphoreType.DMA((13,)),
             pltpu.VMEM((SUB, LANES), f32),
             pltpu.VMEM((2, SUB, LANES), f32),
+            pltpu.VMEM((4, 4, SUB, LANES), f32),
             pltpu.VMEM((2, rows, SUB, LANES), f32),
             pltpu.VMEM((2, 4 * rows, LANES // 2), f32),
             pltpu.VMEM((2, rows, LANES), f32),

time: 24.2 us -> 24.3 us (level)
  no operation moved by 1% of the time
where the time goes in v2:
time: 24.3 us; the launch traced here: 24.1 us
  Pallas kernels  22.2 us (91%)
  local copies, waits for them, and re-layouts  1.2 us (5%)
  between operations  0.64 us (3%)
    pallas_call x1, Pallas kernels, local(): pl.pallas_call(functools.partial(step_kernel, faces, layers), out_shape=(...  22.2 us
    unnamed x2, local copies, waits for them, and re-layouts  1.2 us

profile of v2, /device:TPU:0, one launch (start us, length us, event | category | flops | bytes accessed | tf_op | source)
XLA Modules:
  0.0 24.1 jit_solution(17524035126969437439)
XLA Ops:
  0.6 22.2 %thermal_step.1 = (f32[2,16,128]{2,1,0:T(8,128)S(1)}, f32[8,128]{1,0:T(8,128)S(1)}) custom-call(f32[2,16,128]{2,1,0:T(8,128)} %bitcast.25, f32[2,16,128]{2,1,0:T(8,128)} %bitcast.26, s32[2,256,128]{2,1,0:T(8,128)} %bitcast.23, f32[2,10,64,128]{3,2,1,0:T(8,128)} %bitcast.22, s32[8,128]{1,0:T(8,128)} %bitcast.28, s32[2,3,8,128]{3,2,1,0:T(8,128)} %bitcast.24, ...), custom_call_target="tpu_custom_call" | custom-call | tf_op jit(solution)/shard_map/thermal_step/pallas_call | solution.py:498
  22.9 0.6 %copy.18 = f32[2,1,1,2048]{3,2,1,0:T(1,128)} copy(f32[2,1,1,2048]{3,2,1,0:T(1,128)S(1)} %bitcast.20) | data formatting | bytes 32768
  23.5 0.6 %copy.19 = f32[1,1024]{1,0:T(1,128)} copy(f32[1,1024]{1,0:T(1,128)S(1)} %bitcast.21) | data formatting | bytes 8192

commit v3 on v2

--- a/solution.py
+++ b/solution.py
@@ -112,19 +112,31 @@
         base = row_spread(staged[kind, c, s : s + 1, :], 16).astype(jnp.bfloat16)
         return jnp.concatenate([base] * (count // 16), axis=0)
 
-    left = [[], []]
+    left = []
     right = []
     for c in range(4):
+        blocks = [[], []]
+        marks = []
         for s in range(SUB):
-            right.append(jnp.where(lane_iota == wide(0, c, s, lanes), one, zero))
+            marks.append(jnp.where(lane_iota == wide(0, c, s, lanes), one, zero))
             hit = line_iota == wide(1, c, s, lines)
             for k in range(2):
-                left[k].append(jnp.where(hit, wide(2 + k, c, s, lines), zero_lines))
-    left = jnp.concatenate([jnp.concatenate(one_piece, axis=1) for one_piece in left], axis=0)
-    right = jnp.concatenate(right, axis=1)
-    sums[body] += lax.dot_general(
+                blocks[k].append(jnp.where(hit, wide(2 + k, c, s, lines), zero_lines))
+        left += [jnp.concatenate(block, axis=1) for block in blocks]
+        right.append(jnp.concatenate(marks, axis=1))
+    left = jnp.concatenate(left, axis=0)
+    right = jnp.concatenate(right, axis=0)
+    both = lax.dot_general(
         left, right, (((1,), (1,)), ((), ())), preferred_element_type=jnp.float32
     )
+    side = 2 * lanes
+    sums[body] += both[: 2 * 2 * lines, :side] + both[2 * 2 * lines :, side:]
+
+
+def staged_total(total, rows):
+    lanes = LANES // 2
+    lines = 2 * rows
+    return join(total[: 2 * lines, :lanes] + total[2 * lines :, lanes:], rows, 2)
 
 
 def element_values(i, table, corners_ref, entries_ref, rows):
@@ -302,9 +314,11 @@
         low = jnp.bitwise_and(match, LANES - 1)
         high = jnp.right_shift(match, 7)
 
-        def look(patch, carry):
+        def look(turn, carry):
             normal, trace = carry
-            for s in range(SUB):
+            for at in range(4 * SUB):
+                patch = turn * 4 + at // SUB
+                s = at % SUB
                 hit = high == patch * SUB + s
                 for_normal = row_spread(pad[patch, 0, s : s + 1, :], SUB)
                 for_trace = row_spread(pad[patch, 1, s : s + 1, :], SUB)
@@ -316,7 +330,7 @@
                 )
             return normal, trace
 
-        normal, trace = lax.fori_loop(0, faces, look, (zeros, zeros))
+        normal, trace = lax.fori_loop(0, faces // 4, look, (zeros, zeros))
         active = flag_ref[...].astype(jnp.float32)
         pressure = active * jnp.maximum(gap_ref[2] + nitsche * (gap_ref[0] - normal - gap_ref[1]), 0.0)
         pressure_ref[...] = pressure
@@ -333,7 +347,8 @@
         @pl.when(i == steps // 8)
         def _():
             pl.semaphore_wait(barrier, faces - 1 + around)
-            lax.fori_loop(1, faces, send_pad, 0)
+            for k in range(1, faces):
+                send_pad(k, 0)
 
         @pl.when(i == chunks)
         def _():
@@ -346,7 +361,8 @@
                 one.wait()
             lax.fori_loop(1, faces, wait_pad, 0)
             rate_faces()
-            lax.fori_loop(1, faces, send_rate, 0)
+            for k in range(1, faces):
+                send_rate(k, 0)
 
         index, out = element_values(i, table, corners_ref, entries_ref, rows)
         add_staged(rows, staged, sums, jnp.maximum(i - 1, 0) // chunks)
@@ -379,7 +395,7 @@
 
     lax.fori_loop(0, 3, finish, 0)
     for body in range(2):
-        residual[body] = join(sums[body], rows, 2)
+        residual[body] = staged_total(sums[body], rows)
     get_rim.wait()
     rim = rim_ref[...]
 
@@ -510,7 +526,7 @@
             pltpu.VMEM((2, SUB, LANES), f32),
             pltpu.VMEM((4, 4, SUB, LANES), f32),
             pltpu.VMEM((2, rows, SUB, LANES), f32),
-            pltpu.VMEM((2, 4 * rows, LANES // 2), f32),
+            pltpu.VMEM((2, 8 * rows, LANES), f32),
             pltpu.VMEM((2, rows, LANES), f32),
             pltpu.VMEM((faces, 2, SUB, LANES), f32),
             pltpu.VMEM((faces * SUB, LANES), f32),

time: 24.3 us -> 23.7 us (0.975)
  Pallas kernels: 22.2 us -> 21.6 us
    pallas_call x1, Pallas kernels: 22.2 us -> 21.6 us  [local(): pl.pallas_call(functools.partial(step_kernel, faces, layers), out_shape=(...]
where the time goes in v3:
time: 23.7 us; the launch traced here: 23.4 us
  Pallas kernels  21.6 us (91%)
  local copies, waits for them, and re-layouts  1.2 us (5%)
  between operations  0.64 us (3%)
    pallas_call x1, Pallas kernels, local(): pl.pallas_call(functools.partial(step_kernel, faces, layers), out_shape=(...  21.6 us
    unnamed x2, local copies, waits for them, and re-layouts  1.2 us

profile of v3, /device:TPU:0, one launch (start us, length us, event | category | flops | bytes accessed | tf_op | source)
XLA Modules:
  0.0 23.4 jit_solution(2193133183187894949)
XLA Ops:
  0.6 21.6 %thermal_step.1 = (f32[2,16,128]{2,1,0:T(8,128)S(1)}, f32[8,128]{1,0:T(8,128)S(1)}) custom-call(f32[2,16,128]{2,1,0:T(8,128)} %bitcast.25, f32[2,16,128]{2,1,0:T(8,128)} %bitcast.26, s32[2,256,128]{2,1,0:T(8,128)} %bitcast.23, f32[2,10,64,128]{3,2,1,0:T(8,128)} %bitcast.22, s32[8,128]{1,0:T(8,128)} %bitcast.28, s32[2,3,8,128]{3,2,1,0:T(8,128)} %bitcast.24, ...), custom_call_target="tpu_custom_call" | custom-call | tf_op jit(solution)/shard_map/thermal_step/pallas_call | solution.py:514
  22.2 0.6 %copy.18 = f32[2,1,1,2048]{3,2,1,0:T(1,128)} copy(f32[2,1,1,2048]{3,2,1,0:T(1,128)S(1)} %bitcast.20) | data formatting | bytes 32768
  22.9 0.6 %copy.19 = f32[1,1024]{1,0:T(1,128)} copy(f32[1,1024]{1,0:T(1,128)S(1)} %bitcast.21) | data formatting | bytes 8192

commit v4 on v3

--- a/solution.py
+++ b/solution.py
@@ -14,6 +14,7 @@
 LANES = 128
 SUB = 8
 MESH = pl.DeviceIdType.MESH
+GROUP = 2
 
 
 def row_spread(row, count):
@@ -90,13 +91,14 @@
         table[body, r] = row_spread(field_ref[body, r : r + 1, :], SUB)
 
 
-def stage(c, index, value, rows, staged):
+def stage(c, u, index, value, rows, staged):
+    here = slice(u * SUB, (u + 1) * SUB)
     half = jnp.bitwise_and(jnp.right_shift(index, 6), 1) * rows
-    staged[0, c] = jnp.bitwise_and(index, LANES // 2 - 1).astype(jnp.float32)
-    staged[1, c] = (jnp.right_shift(index, 7) + half).astype(jnp.float32)
+    staged[0, c, here] = jnp.bitwise_and(index, LANES // 2 - 1).astype(jnp.float32)
+    staged[1, c, here] = (jnp.right_shift(index, 7) + half).astype(jnp.float32)
     head = value.astype(jnp.bfloat16).astype(jnp.float32)
-    staged[2, c] = head
-    staged[3, c] = value - head
+    staged[2, c, here] = head
+    staged[3, c, here] = value - head
 
 
 def add_staged(rows, staged, sums, body):
@@ -117,7 +119,7 @@
     for c in range(4):
         blocks = [[], []]
         marks = []
-        for s in range(SUB):
+        for s in range(GROUP * SUB):
             marks.append(jnp.where(lane_iota == wide(0, c, s, lanes), one, zero))
             hit = line_iota == wide(1, c, s, lines)
             for k in range(2):
@@ -139,10 +141,7 @@
     return join(total[: 2 * lines, :lanes] + total[2 * lines :, lanes:], rows, 2)
 
 
-def element_values(i, table, corners_ref, entries_ref, rows):
-    chunks = entries_ref.shape[2] // SUB
-    body = i // chunks
-    j = lax.rem(i, chunks)
+def element_values(body, j, table, corners_ref, entries_ref, rows):
     first = pl.multiple_of(j * (4 * SUB), 4 * SUB)
     tile = pl.multiple_of(j * SUB, SUB)
     index = [corners_ref[body, pl.ds(first + c, SUB, stride=4), :] for c in range(4)]
@@ -340,8 +339,8 @@
 
     get_corners[0].wait()
     get_entries[0].wait()
-    chunks = entries_ref.shape[2] // SUB
-    steps = 2 * chunks
+    turns = entries_ref.shape[2] // (GROUP * SUB)
+    steps = 2 * turns
 
     def run(i, carry):
         @pl.when(i == steps // 8)
@@ -350,7 +349,7 @@
             for k in range(1, faces):
                 send_pad(k, 0)
 
-        @pl.when(i == chunks)
+        @pl.when(i == turns)
         def _():
             get_corners[1].wait()
             get_entries[1].wait()
@@ -364,10 +363,16 @@
             for k in range(1, faces):
                 send_rate(k, 0)
 
-        index, out = element_values(i, table, corners_ref, entries_ref, rows)
-        add_staged(rows, staged, sums, jnp.maximum(i - 1, 0) // chunks)
-        for c in range(4):
-            stage(c, index[c], out[c], rows, staged)
+        made = [
+            element_values(
+                i // turns, lax.rem(i, turns) * GROUP + u, table, corners_ref, entries_ref, rows
+            )
+            for u in range(GROUP)
+        ]
+        add_staged(rows, staged, sums, jnp.maximum(i - 1, 0) // turns)
+        for u, (index, out) in enumerate(made):
+            for c in range(4):
+                stage(c, u, index[c], out[c], rows, staged)
         return carry
 
     lax.fori_loop(0, steps, run, 0)
@@ -381,21 +386,16 @@
     rates[1] = -lax.fori_loop(1, faces, wait_rate, own)
     surface = (layer == 0).astype(jnp.float32)
 
-    def finish(k, carry):
-        add_staged(rows, staged, sums, lax.rem(k + 1, 2))
-
-        @pl.when(k < 2)
-        def _():
-            share = surface * rates[k] / 3.0
-            for c in range(3):
-                stage(c, tri_ref[k, c], share, rows, staged)
-            stage(3, tri_ref[k, 0], zeros, rows, staged)
-
-        return carry
-
-    lax.fori_loop(0, 3, finish, 0)
+    add_staged(rows, staged, sums, 1)
+    at_faces = []
+    shares = []
     for body in range(2):
-        residual[body] = staged_total(sums[body], rows)
+        share = surface * rates[body] / 3.0
+        at_faces += [tri_ref[body, c] + body * rows * LANES for c in range(3)]
+        shares += [share] * 3
+    contact = join(add_into(at_faces, shares, 2 * rows, 2), 2 * rows, 2)
+    for body in range(2):
+        residual[body] = staged_total(sums[body], rows) + contact[body * rows : (body + 1) * rows]
     get_rim.wait()
     rim = rim_ref[...]
 
@@ -524,7 +524,7 @@
             pltpu.SemaphoreType.DMA((13,)),
             pltpu.VMEM((SUB, LANES), f32),
             pltpu.VMEM((2, SUB, LANES), f32),
-            pltpu.VMEM((4, 4, SUB, LANES), f32),
+            pltpu.VMEM((4, 4, GROUP * SUB, LANES), f32),
             pltpu.VMEM((2, rows, SUB, LANES), f32),
             pltpu.VMEM((2, 8 * rows, LANES), f32),
             pltpu.VMEM((2, rows, LANES), f32),

time: 23.7 us -> 23.5 us (level)
  no operation moved by 1% of the time
where the time goes in v4:
time: 23.5 us; the launch traced here: 23.2 us
  Pallas kernels  21.4 us (91%)
  local copies, waits for them, and re-layouts  1.2 us (5%)
  between operations  0.64 us (3%)
    pallas_call x1, Pallas kernels, local(): pl.pallas_call(functools.partial(step_kernel, faces, layers), out_shape=(...  21.4 us
    unnamed x2, local copies, waits for them, and re-layouts  1.2 us

profile of v4, /device:TPU:0, one launch (start us, length us, event | category | flops | bytes accessed | tf_op | source)
XLA Modules:
  0.0 23.2 jit_solution(1084110600253870837)
XLA Ops:
  0.6 21.4 %thermal_step.1 = (f32[2,16,128]{2,1,0:T(8,128)S(1)}, f32[8,128]{1,0:T(8,128)S(1)}) custom-call(f32[2,16,128]{2,1,0:T(8,128)} %bitcast.25, f32[2,16,128]{2,1,0:T(8,128)} %bitcast.26, s32[2,256,128]{2,1,0:T(8,128)} %bitcast.23, f32[2,10,64,128]{3,2,1,0:T(8,128)} %bitcast.22, s32[8,128]{1,0:T(8,128)} %bitcast.28, s32[2,3,8,128]{3,2,1,0:T(8,128)} %bitcast.24, ...), custom_call_target="tpu_custom_call" | custom-call | tf_op jit(solution)/shard_map/thermal_step/pallas_call | solution.py:514
  22.0 0.6 %copy.18 = f32[2,1,1,2048]{3,2,1,0:T(1,128)} copy(f32[2,1,1,2048]{3,2,1,0:T(1,128)S(1)} %bitcast.20) | data formatting | bytes 32768
  22.6 0.6 %copy.19 = f32[1,1024]{1,0:T(1,128)} copy(f32[1,1024]{1,0:T(1,128)S(1)} %bitcast.21) | data formatting | bytes 8192

commit v5 on v4

--- a/solution.py
+++ b/solution.py
@@ -343,7 +343,7 @@
     steps = 2 * turns
 
     def run(i, carry):
-        @pl.when(i == steps // 8)
+        @pl.when(i == 0)
         def _():
             pl.semaphore_wait(barrier, faces - 1 + around)
             for k in range(1, faces):
@@ -354,7 +354,7 @@
             get_corners[1].wait()
             get_entries[1].wait()
 
-        @pl.when(i == steps * 5 // 8)
+        @pl.when(i == steps * 3 // 8)
         def _():
             for one in get_rest:
                 one.wait()

time: 23.5 us -> 23.5 us (level)
  no operation moved by 1% of the time
where the time goes in v5:
time: 23.5 us; the launch traced here: 23.2 us
  Pallas kernels  21.4 us (91%)
  local copies, waits for them, and re-layouts  1.2 us (5%)
  between operations  0.64 us (3%)
    pallas_call x1, Pallas kernels, local(): pl.pallas_call(functools.partial(step_kernel, faces, layers), out_shape=(...  21.4 us
    unnamed x2, local copies, waits for them, and re-layouts  1.2 us

profile of v5, /device:TPU:0, one launch (start us, length us, event | category | flops | bytes accessed | tf_op | source)
XLA Modules:
  0.0 23.2 jit_solution(9203634951475524554)
XLA Ops:
  0.6 21.4 %thermal_step.1 = (f32[2,16,128]{2,1,0:T(8,128)S(1)}, f32[8,128]{1,0:T(8,128)S(1)}) custom-call(f32[2,16,128]{2,1,0:T(8,128)} %bitcast.25, f32[2,16,128]{2,1,0:T(8,128)} %bitcast.26, s32[2,256,128]{2,1,0:T(8,128)} %bitcast.23, f32[2,10,64,128]{3,2,1,0:T(8,128)} %bitcast.22, s32[8,128]{1,0:T(8,128)} %bitcast.28, s32[2,3,8,128]{3,2,1,0:T(8,128)} %bitcast.24, ...), custom_call_target="tpu_custom_call" | custom-call | tf_op jit(solution)/shard_map/thermal_step/pallas_call | solution.py:514
  22.0 0.6 %copy.18 = f32[2,1,1,2048]{3,2,1,0:T(1,128)} copy(f32[2,1,1,2048]{3,2,1,0:T(1,128)S(1)} %bitcast.20) | data formatting | bytes 32768
  22.6 0.6 %copy.19 = f32[1,1024]{1,0:T(1,128)} copy(f32[1,1024]{1,0:T(1,128)S(1)} %bitcast.21) | data formatting | bytes 8192
